TPU v7x, 512 devices: a whole 4x8x8 slice. The times are simulated.
512 devices in a mesh: seq: 16 (over z_hi, x, core), head: 32 (over z_lo, y).
Axes of the slice: x: 4, y: 8, z: 8 (z_hi: 2, z_lo: 4; z = z_hi * 4 + z_lo), core: 2. Of those that a mesh axis runs over, the one named last changes fastest.
Arguments:
- queries: bfloat16 [4096, 16384], P('seq', 'head'), may hold values from -100 to 100
- key_rows: bfloat16 [4096, 1024], P('seq'), may hold values from -4 to 4
- value_rows: bfloat16 [4096, 1024], P('seq'), may hold values from -6 to 6
- value_turn: bfloat16 [8, 128, 128], replicated, may hold values from -0.5 to 0.5
- block_map: int32 [128], replicated, may hold values from 0 to 127, each once
- block_turn: bfloat16 [128, 128, 128], P('head'), may hold values from -0.5 to 0.5
- out_weight: bfloat16 [16384, 8192], P('head', 'seq'), may hold values from -1.5 to 1.5
Outputs:
- mixed: bfloat16 [8192, 4096], P('head', 'seq')
Inputs may be any that keep to these rules, and one draw needn't show every extreme that they name: `block_map`: every block position 0 to 127 appears once.
All inputs are finite; a program needn't handle non-finite values.
Results may differ from a plain program's by a relative error of at most 0.03.
Values may be sent and summed in bfloat16 or wider, within the bound.
A program may use at most 128 MiB of HBM per device.

v0:
```python
import jax
import jax.numpy as jnp
from jax import lax
from jax.sharding import PartitionSpec as P

GROUP = 16


def on_device(queries, key_rows, value_rows, value_turn, block_map, block_turn, out_weight):
    tok_count = queries.shape[0]
    head_dim = value_turn.shape[1]
    per_dev = queries.shape[1] // head_dim
    heads_total = block_map.shape[0]
    seq_place = lax.axis_index("seq")
    head_place = lax.axis_index("head")
    group = head_place * per_dev // GROUP
    key_local = lax.dynamic_slice_in_dim(key_rows, group * head_dim, head_dim, 1)
    value_local = lax.dynamic_slice_in_dim(value_rows, group * head_dim, head_dim, 1)
    turn = lax.dynamic_index_in_dim(value_turn, group, 0, keepdims=False)
    value_turned = jnp.dot(value_local, turn, preferred_element_type=jnp.float32).astype(
        jnp.bfloat16
    )
    query_flat = queries.reshape(tok_count * per_dev, head_dim)
    query_pos = seq_place * tok_count + jnp.arange(tok_count * per_dev, dtype=jnp.int32) // per_dev
    scale = 1.0 / head_dim**0.5
    row_count = tok_count * per_dev
    top_old = jnp.full((row_count,), -1e30, jnp.float32)
    key_piece = lax.all_gather(key_local, "seq", axis=0, tiled=True)
    value_piece = lax.all_gather(value_turned, "seq", axis=0, tiled=True)
    scores = (
        lax.dot_general(
            query_flat, key_piece, (((1,), (1,)), ((), ())), preferred_element_type=jnp.float32
        )
        * scale
    )
    key_pos = jnp.arange(key_piece.shape[0], dtype=jnp.int32)
    allowed = key_pos[None, :] <= query_pos[:, None]
    top_new = jnp.maximum(top_old, jnp.max(jnp.where(allowed, scores, jnp.float32(-1e30)), axis=1))
    weights = jnp.where(allowed, jnp.exp(scores - top_new[:, None]), jnp.float32(0.0))
    total_new = jnp.sum(weights, axis=1)
    summed_new = jnp.dot(
        weights.astype(jnp.bfloat16), value_piece, preferred_element_type=jnp.float32
    )
    attended = (
        (summed_new / total_new[:, None])
        .astype(jnp.bfloat16)
        .reshape(tok_count, per_dev * head_dim)
    )
    every = lax.all_gather(attended, "head", axis=1, tiled=True)
    targets = head_place * per_dev + jnp.arange(per_dev, dtype=jnp.int32)
    select = (block_map[:, None] == targets[None, :]).astype(jnp.bfloat16)
    mine = jnp.einsum(
        "tbc,bi->tic",
        every.reshape(tok_count, heads_total, head_dim),
        select,
        preferred_element_type=jnp.float32,
    ).astype(jnp.bfloat16)
    rotated = jnp.einsum(
        "tic,icd->tid", mine, block_turn, preferred_element_type=jnp.float32
    ).astype(jnp.bfloat16)
    rotated = rotated.reshape(tok_count, per_dev * head_dim)
    columns = lax.all_gather(out_weight, "seq", axis=1, tiled=True)
    return lax.psum_scatter(
        lax.dot_general(
            columns, rotated, (((0,), (1,)), ((), ())), preferred_element_type=jnp.float32
        ).astype(jnp.bfloat16),
        "head",
        scatter_dimension=0,
        tiled=True,
    )


def solution(mesh):
    placed = (
        P("seq", "head"),
        P("seq", None),
        P("seq", None),
        P(),
        P(),
        P("head", None, None),
        P("head", "seq"),
    )
    return jax.shard_map(
        on_device, mesh=mesh, in_specs=placed, out_specs=P("head", "seq"), check_vma=False
    )
```

profile of v0, /device:TPU:2, one launch (start us, length us, event | category | flops | bytes accessed | tf_op | source)
XLA Modules:
  0.0 613.1 jit_solution(7639849423053635896)
XLA Ops:
  6.5 0.0 copy-start
  6.5 0.0 all-gather.5.cloned.1.call-start
  6.5 1.0 copy-done
  7.6 0.6 constant_dynamic-slice_fusion
  8.2 0.0 all-gather.5.cloned.1.call-update
  8.2 0.0 all-gather.7.cloned.1.call-start
  8.3 1.6 convolution_convert_fusion.2
  9.9 0.0 all-gather.7.cloned.1.call-update
  9.9 0.0 all-gather.9.cloned.1.call-start
  10.0 1.1 reshape.35
  11.1 65.5 %all-gather.5.cloned.1.call-done = bf16[4096,128]{1,0:T(8,128)(2,1)} async-done(((bf16[256,128]{1,0:T(8,128)(2,1)}), bf16[4096,128]{1,0:T(8,128)(2,1)}) %all-gather.5.cloned.1.call-update) | async-done | bytes 1048592 | tf_op jit(solution)/shard_map/all_gather | solution.py:28
  76.6 4.1 fusion
  80.7 0.0 copy-start.1
  80.7 5.7 copy-done.1
  86.5 4.4 fusion.3
  90.9 46.3 %all-gather.7.cloned.1.call-done = bf16[4096,128]{1,0:T(8,128)(2,1)} async-done(((bf16[256,128]{1,0:T(8,128)(2,1)}), bf16[4096,128]{1,0:T(8,128)(2,1)}) %all-gather.7.cloned.1.call-update) | async-done | bytes 1048592 | tf_op jit(solution)/shard_map/all_gather | solution.py:29
  137.2 10.0 %fusion.11 = bf16[1024,128]{1,0:T(8,128)(2,1)S(1)} fusion(bf16[4096,128]{1,0:T(8,128)(2,1)} %all-gather.7.cloned.1.call-done, f32[4096,1024]{1,0:T(8,128)} %copy-done.1, f32[1024]{0:T(1024)S(1)} %broadcast_maximum_fusion, s32[1024]{0:T(1024)S(1)} %fusion.24, f32[1024]{0:T(1024)S(1)} %fusion.3), kind=kOutput, calls=%fused_computation.14 | convolution fusion | flops 1094975488 | bytes 18100224 | tf_op jit(solution)/shard_map/dot_general | solution.py:41
  147.3 0.0 copy-start.3
  147.3 0.9 reshape.36
  148.1 0.0 all-gather.9.cloned.1.call-update
  148.2 0.0 all-gather.11.cloned.1.call-start
  148.2 0.5 all-gather.11.cloned.1.call-update
  148.7 0.2 reduce-scatter.2.cloned.1.call-start
  149.0 165.2 %all-gather.9.cloned.1.call-done = bf16[256,16384]{1,0:T(8,128)(2,1)} async-done(((bf16[256,512]{1,0:T(8,128)(2,1)}), bf16[256,16384]{1,0:T(8,128)(2,1)}) %all-gather.9.cloned.1.call-update) | async-done | bytes 8388624 | tf_op jit(solution)/shard_map/all_gather | solution.py:49
  314.2 0.0 copy-start.2
  314.2 9.2 %copy.12 = bf16[32,8,128,128]{3,2,1,0:T(8,128)(2,1)} copy(bf16[32,8,128,128]{3,1,2,0:T(8,128)(2,1)} %bitcast.42) | data formatting | bytes 16777216
  323.4 0.0 copy-done.3
  323.4 4.7 fusion.17
  328.1 0.0 copy-done.2
  328.1 0.3 convolution_convert_fusion.1
  328.4 103.0 %all-gather.11.cloned.1.call-done = bf16[512,8192]{1,0:T(8,128)(2,1)} async-done(((bf16[512,512]{1,0:T(8,128)(2,1)}), bf16[512,8192]{1,0:T(8,128)(2,1)}) %all-gather.11.cloned.1.call-update) | async-done | bytes 8388624 | tf_op jit(solution)/shard_map/all_gather | solution.py:62
  431.5 7.7 %fusion.5 = bf16[8192,256]{0,1:T(8,128)(2,1)} fusion(bf16[256,512]{0,1:T(8,128)(2,1)S(1)} %bitcast.43, bf16[512,8192]{1,0:T(8,128)(2,1)} %all-gather.11.cloned.1.call-done), kind=kOutput, calls=%fused_computation.9 | convolution fusion | flops 2149580800 | bytes 12845056 | tf_op jit(solution)/shard_map/dot_general | solution.py:64
  439.2 0.0 reduce-scatter.2.cloned.1.call-update
  439.2 165.7 %reduce-scatter.2.cloned.1.call-done = bf16[256,256]{0,1:T(8,128)(2,1)} async-done(((bf16[8192,256]{0,1:T(8,128)(2,1)}), bf16[256,256]{0,1:T(8,128)(2,1)}) %reduce-scatter.2.cloned.1.call-update) | async-done | bytes 131088 | tf_op jit(solution)/shard_map/reduce_scatter | solution.py:63
  604.9 1.7 copy.9
  (3 shorter events, 0.0 us)
Async XLA Ops:
  6.5 1.0 copy-start
  6.5 70.1 %all-gather.5.cloned.1.call-start = ((), (), s32[]{:S(2)}) async-start(), calls=%async_computation.1 | async-start | bytes 1114112 | tf_op jit(solution)/shard_map/all_gather | solution.py:28
  8.2 129.0 %all-gather.7.cloned.1.call-start = ((), (), s32[]{:S(2)}) async-start(), calls=%async_computation.2 | async-start | bytes 1114112 | tf_op jit(solution)/shard_map/all_gather | solution.py:29
  9.9 304.3 %all-gather.9.cloned.1.call-start = ((), (), s32[]{:S(2)}) async-start(), calls=%async_computation.3 | async-start | bytes 8650752 | tf_op jit(solution)/shard_map/all_gather | solution.py:49
  80.7 5.7 copy-start.1
  147.3 176.2 %copy-start.3 = (s32[128]{0:T(128)S(1)}, s32[128]{0:T(128)}, u32[]{:S(2)}) copy-start(s32[128]{0:T(128)} %param.11) | copy-start | bytes 1540
  148.2 283.3 %all-gather.11.cloned.1.call-start = ((), (), s32[]{:S(2)}) async-start(), calls=%async_computation.4 | async-start | bytes 8912896 | tf_op jit(solution)/shard_map/all_gather | solution.py:62
  148.7 456.1 %reduce-scatter.2.cloned.1.call-start = ((), (), s32[]{:S(2)}) async-start(), calls=%async_computation.5 | async-start | bytes 4325376 | tf_op jit(solution)/shard_map/reduce_scatter | solution.py:63
  314.2 13.9 %copy-start.2 = (bf16[4,128,128]{2,1,0:T(8,128)(2,1)S(1)}, bf16[4,128,128]{2,1,0:T(8,128)(2,1)}, u32[]{:S(2)}) copy-start(bf16[4,128,128]{2,1,0:T(8,128)(2,1)} %param.12) | copy-start | bytes 393220
Sparse Core Ops, SparseCore 0:
  10.7 65.9 all-gather.4
  80.0 57.1 all-gather.6
  148.3 165.8 all-gather.8
  317.2 114.2 all-gather.10
  439.3 165.5 reduce-scatter.1
where the time goes:
time: 613 us
  waiting for transfers between devices  546 us (89%)
  matrix products  28.4 us (5%)
  local copies, waits for them, and re-layouts  20.3 us (3%)
  between operations  13.2 us (2%)
    reduce_scatter x1, waiting for transfers between devices, on_device(): lax.psum_scatter(lax.dot_general(columns, rotated, (((0,), (1,)), ((), ()...  166 us
    all_gather x1, waiting for transfers between devices, on_device(): every = lax.all_gather(attended, 'head', axis=1, tiled=True)  165 us
    all_gather x1, waiting for transfers between devices, on_device(): columns = lax.all_gather(out_weight, 'seq', axis=1, tiled=True)  103 us
    all_gather x1, waiting for transfers between devices, on_device(): key_piece = lax.all_gather(key_local, 'seq', axis=0, tiled=True)  65.5 us
    all_gather x1, waiting for transfers between devices, on_device(): value_piece = lax.all_gather(value_turned, 'seq', axis=0, tiled=True)  46.3 us
    unnamed x9, local copies, waits for them, and re-layouts  16 us
  transfers between devices with their start and end apart: 5, of which 5 were waited for; matrix products, arithmetic and copies ran while one was open for 4% of the time, Pallas kernels for 0%

commit v1 on v0

v1 whole, which is shorter than its diff:
```python
import functools
import math

import jax
import jax.numpy as jnp
from jax import lax
from jax.experimental import pallas as pl
from jax.experimental.pallas import tpu as pltpu
from jax.sharding import PartitionSpec as P

MESH = pl.DeviceIdType.MESH
BF = jnp.bfloat16
F32 = jnp.float32
HD = 128
TOK = 256


def dev(zh, x, c, zl, y):
    return (zh * 8 + x * 2 + c, zl * 8 + y)


def send(src, dst, ssem, rsem, to):
    copy = pltpu.make_async_remote_copy(
        src_ref=src, dst_ref=dst, send_sem=ssem, recv_sem=rsem, device_id=to, device_id_type=MESH
    )
    copy.start()
    return copy


def arrived(slot, sem):
    pltpu.make_async_copy(slot, slot, sem).wait()


def kernel(
    map_ref, q_ref, key_ref, val_ref, vturn_ref, bturn_ref, w_ref, out_ref,
    kv, q_all, score, att, wst, w1, w2s, wfull, a_st, a_full, cst, cin,
    kc_s, kx_s, kx_r, kc_r, kd_s, kd_r, kxx_s, kxx_r,
    w1_s, w1_r, w2_s, w2_r, wx_s, wx_r, wd_s, wd_r,
    ac_s, ac_r, rr_s, rr_r, ll_s, ll_r, c_s, c_r,
):
    s = lax.axis_index("seq")
    h = lax.axis_index("head")
    zh, x, c = s // 8, (s // 2) % 4, s % 2
    zl, y = h // 8, h % 8
    z = zh * 4 + zl

    g = zl * 2 + y // 4
    lanes = pl.ds(pl.multiple_of(g * HD, HD), HD)
    kv[s, 0] = key_ref[:, lanes]
    kv[s, 1] = jnp.dot(val_ref[:, lanes], vturn_ref[g], preferred_element_type=F32).astype(BF)

    @pl.when(zh == 0)
    def _():
        send(kv.at[s], kv.at[s], kc_s, kc_r, dev(1, x, c, zl, y))

    for off in (1, 2, 3):
        @pl.when(x + off < 4)
        def _():
            send(kv.at[s], kv.at[s], kx_s.at[off], kx_r.at[x], dev(zh, x + off, c, zl, y))

    @pl.when(c == 0)
    def _():
        send(kv.at[s], kv.at[s], kd_s.at[zh * 4 + x], kd_r.at[zh * 4 + x], dev(zh, x, 1, zl, y))

    for i in range(4):
        turned = lax.dot_general(
            w_ref[i * HD:(i + 1) * HD, :], bturn_ref[i], (((0,), (1,)), ((), ())), preferred_element_type=F32
        ).astype(BF)
        wst[:, i] = turned.reshape(32, 16, HD)
    x_to = (x + zh) % 4

    def w1_place(n):
        r, m = n // 16, n % 16
        cq, zq = m // 8, m % 8
        return dev(zq // 4, x_to, cq, zq % 4, 4 * (x % 2) + 2 * c + r)

    def w1_send(step, carry):
        n = (step + h) % 32
        to = w1_place(n)
        mine = (to[0] == s) & (to[1] == h)

        @pl.when(jnp.logical_not(mine))
        def _():
            send(wst.at[n], w1.at[pl.ds(h * 4, 4)], w1_s.at[n], w1_r.at[h], to)

        @pl.when(mine)
        def _():
            pltpu.make_async_copy(wst.at[n], w1.at[pl.ds(h * 4, 4)], w1_r.at[h]).start()

        return carry

    lax.fori_loop(0, 32, w1_send, 0)

    @pl.when(zh == 1)
    def _():
        arrived(kv.at[s - 8], kc_r)
        for off in (1, 2, 3):
            send(kv.at[s - 8], kv.at[s - 8], kxx_s.at[off], kxx_r.at[off], dev(1, (x + off) % 4, c, zl, y))
        send(kv.at[s - 8], kv.at[s - 8], kd_s.at[x], kd_r.at[x], dev(1, x, 1 - c, zl, y))

    for xs in range(3):
        @pl.when(xs < x)
        def _():
            slot = kv.at[zh * 8 + xs * 2 + c]
            arrived(slot, kx_r.at[xs])
            send(slot, slot, kd_s.at[zh * 4 + xs], kd_r.at[zh * 4 + xs], dev(zh, x, 1 - c, zl, y))

    @pl.when(zh == 1)
    def _():
        for off in (1, 2, 3):
            xs = (x + 4 - off) % 4
            slot = kv.at[xs * 2 + c]
            arrived(slot, kxx_r.at[off])
            send(slot, slot, kd_s.at[xs], kd_r.at[xs], dev(1, x, 1 - c, zl, y))

    for hh in range(32):
        arrived(w1.at[pl.ds(hh * 4, 4)], w1_r.at[hh])

    def held_rows(xx):
        zs = (xx + y // 4) % 2
        xs = (xx + 4 - zs) % 4
        return pl.multiple_of((2 * zs + xs // 2) * 256 + c * 128, 128)

    rows = held_rows(x)
    my_rows = pl.ds(pl.multiple_of(rows + z * 16, 16), 16)

    def w2_send(step, carry):
        zt = (z + step) % 8
        zht, zlt = zt // 4, zt % 4
        for kk in range(16):
            block = map_ref[(zlt * 8 + kk // 2) * 4 + zht * 2 + kk % 2]
            w2s[step, :, kk * HD:(kk + 1) * HD] = w1[block]

        @pl.when(step > 0)
        def _():
            send(w2s.at[step], wfull.at[my_rows, :], w2_s.at[step], w2_r.at[z], dev(zht, x, c, zlt, y))

        @pl.when(step == 0)
        def _():
            pltpu.make_async_copy(w2s.at[step], wfull.at[my_rows, :], w2_r.at[z]).start()

        return carry

    lax.fori_loop(0, 8, w2_send, 0)

    for xs in range(4):
        @pl.when((xs < x) | ((xs == x) & (c == 1)))
        def _():
            arrived(kv.at[zh * 8 + xs * 2 + 1 - c], kd_r.at[zh * 4 + xs])

        @pl.when(zh == 1)
        def _():
            arrived(kv.at[xs * 2 + 1 - c], kd_r.at[xs])

    for i in range(4):
        q_all[i * TOK:(i + 1) * TOK, :] = q_ref[:, i * HD:(i + 1) * HD]
    turn = math.log2(math.e) / math.sqrt(HD)

    def scored(i, u):
        return lax.dot_general(
            q_all[i * TOK:(i + 1) * TOK, :], kv[u, 0], (((1,), (1,)), ((), ())), preferred_element_type=F32
        )

    seen = lax.broadcasted_iota(jnp.int32, (TOK, TOK), 1) <= lax.broadcasted_iota(jnp.int32, (TOK, TOK), 0)
    for i in range(4):
        own = jnp.where(seen, scored(i, s), F32(-1e30))
        score[s] = own

        def first(u, top, i=i):
            value = scored(i, u)
            score[u] = value
            return jnp.maximum(top, jnp.maximum(value[:, :HD], value[:, HD:]))

        top = lax.fori_loop(0, s, first, jnp.maximum(own[:, :HD], own[:, HD:]))
        top = jnp.max(top, axis=1, keepdims=True) * turn

        def second(u, carry, top=top):
            total, acc = carry
            weight = jnp.exp2(score[u] * turn - top)
            total = total + weight[:, :HD] + weight[:, HD:]
            acc = acc + jnp.dot(weight.astype(BF), kv[u, 1], preferred_element_type=F32)
            return total, acc

        zero = jnp.zeros((TOK, HD), F32)
        total, acc = lax.fori_loop(0, s + 1, second, (zero, zero))
        att[i // 2, :, (i % 2) * HD:(i % 2 + 1) * HD] = (acc / jnp.sum(total, axis=1, keepdims=True)).astype(BF)

    a_full[y, zh] = att[zh]
    a_st[...] = att[1 - zh]
    send(a_st, a_full.at[y, zh], ac_s, ac_r, dev(1 - zh, x, c, zl, y))
    right = dev(zh, x, c, zl, (y + 1) % 8)
    left = dev(zh, x, c, zl, (y + 7) % 8)

    def part(slot, p):
        return a_full.at[slot % 8, zh if p == 0 else 1 - zh]

    def go(k, p):
        if k < 3 or p == 0:
            ref = part(y + 8 - k, p)
            send(ref, ref, rr_s.at[k, p], rr_r.at[k, p], right)
        if k < 3 or p == 1:
            ref = part(y + k, p)
            send(ref, ref, ll_s.at[k, p], ll_r.at[k, p], left)

    go(0, 0)

    for zq in range(8):
        arrived(wfull.at[pl.ds(pl.multiple_of(rows + zq * 16, 16), 16), :], w2_r.at[zq])
    chunk = wfull.at[pl.ds(rows, 128), :]
    for off in (1, 2, 3):
        send(chunk, chunk, wx_s.at[off], wx_r.at[off], dev(zh, (x + off) % 4, c, zl, y))
    send(chunk, chunk, wd_s.at[0], wd_r.at[0], dev(zh, x, 1 - c, zl, y))

    arrived(part(y, 1), ac_r)
    go(0, 1)
    for k in (1, 2, 3):
        for p in (0, 1):
            arrived(part(y + 8 - k, p), rr_r.at[k - 1, p])
            arrived(part(y + k, p), ll_r.at[k - 1, p])
            go(k, p)

    for off in (1, 3, 2):
        theirs = wfull.at[pl.ds(held_rows((x + 4 - off) % 4), 128), :]
        arrived(theirs, wx_r.at[off])
        send(theirs, theirs, wd_s.at[off], wd_r.at[off], dev(zh, x, 1 - c, zl, y))
    for off in (0, 1, 3, 2):
        other = held_rows((x + 4 - off) % 4) + 128 - 256 * c
        arrived(wfull.at[pl.ds(pl.multiple_of(other, 128), 128), :], wd_r.at[off])

    arrived(part(y + 4, 0), rr_r.at[3, 0])
    arrived(part(y + 4, 1), ll_r.at[3, 1])

    def piece(step, carry):
        half = (step + 1) // 2
        d = jnp.where(step % 2 == 1, 4 + half, 12 - half) % 8
        zt = (z + d) % 8
        zht, zlt = zt // 4, zt % 4
        cols = pl.ds(pl.multiple_of(zlt * 256, 256), 256)
        acc = jnp.zeros((256, TOK), F32)
        for yy in range(8):
            acc = acc + lax.dot_general(
                wfull[cols, yy * 256:(yy + 1) * 256], a_full[yy, zht], (((1,), (1,)), ((), ())),
                preferred_element_type=F32,
            )

        @pl.when(d > 0)
        def _():
            cst[d] = acc.astype(BF)
            send(cst.at[d], cin.at[z], c_s.at[d], c_r.at[z], dev(zht, x, c, zlt, y))

        @pl.when(d == 0)
        def _():
            cst[0] = acc.astype(BF)

        return carry

    lax.fori_loop(0, 8, piece, 0)
    total = cst[0].astype(F32)
    for d in range(1, 8):
        zs = (z + d) % 8
        arrived(cin.at[zs], c_r.at[zs])
        total = total + cin[zs].astype(F32)
    out_ref[...] = total.astype(BF)

    @pl.when(zh == 0)
    def _():
        arrived(kv.at[s], kc_s)

    for off in (1, 2, 3):
        @pl.when(x + off < 4)
        def _():
            arrived(kv.at[s], kx_s.at[off])

        @pl.when(zh == 1)
        def _():
            arrived(kv.at[s - 8], kxx_s.at[off])

    for xs in range(4):
        @pl.when((xs < x) | ((xs == x) & (c == 0)))
        def _():
            arrived(kv.at[s], kd_s.at[zh * 4 + xs])

        @pl.when(zh == 1)
        def _():
            arrived(kv.at[s], kd_s.at[xs])

    def w1_sent(n, carry):
        to = w1_place(n)

        @pl.when(jnp.logical_not((to[0] == s) & (to[1] == h)))
        def _():
            arrived(wst.at[n], w1_s.at[n])

        return carry

    lax.fori_loop(0, 32, w1_sent, 0)
    for d in range(1, 8):
        arrived(w2s.at[d], w2_s.at[d])
        arrived(cst.at[d], c_s.at[d])
    for off in (1, 2, 3):
        arrived(chunk, wx_s.at[off])
    for off in range(4):
        arrived(chunk, wd_s.at[off])
    arrived(a_st, ac_s)
    for k in range(4):
        for p in (0, 1):
            if k < 3 or p == 0:
                arrived(part(y, 0), rr_s.at[k, p])
            if k < 3 or p == 1:
                arrived(part(y, 0), ll_s.at[k, p])


def on_device(queries, key_rows, value_rows, value_turn, block_map, block_turn, out_weight):
    vmem = pl.BlockSpec(memory_space=pltpu.VMEM)
    dma = pltpu.SemaphoreType.DMA
    return pl.pallas_call(
        kernel,
        out_shape=jax.ShapeDtypeStruct((256, TOK), BF),
        in_specs=[pl.BlockSpec(memory_space=pltpu.SMEM)] + [vmem] * 6,
        out_specs=vmem,
        scratch_shapes=[
            pltpu.VMEM((16, 2, TOK, HD), BF),
            pltpu.VMEM((4 * TOK, HD), BF),
            pltpu.VMEM((16, TOK, TOK), F32),
            pltpu.VMEM((2, TOK, 256), BF),
            pltpu.VMEM((32, 4, 16, HD), BF),
            pltpu.VMEM((128, 16, HD), BF),
            pltpu.VMEM((8, 16, 2048), BF),
            pltpu.VMEM((1024, 2048), BF),
            pltpu.VMEM((TOK, 256), BF),
            pltpu.VMEM((8, 2, TOK, 256), BF),
            pltpu.VMEM((8, 256, TOK), BF),
            pltpu.VMEM((8, 256, TOK), BF),
            dma(()), dma((4,)), dma((4,)), dma(()), dma((8,)), dma((8,)), dma((4,)), dma((4,)),
            dma((32,)), dma((32,)), dma((8,)), dma((8,)), dma((4,)), dma((4,)), dma((4,)), dma((4,)),
            dma(()), dma(()), dma((4, 2)), dma((4, 2)), dma((4, 2)), dma((4, 2)), dma((8,)), dma((8,)),
        ],
        compiler_params=pltpu.CompilerParams(has_side_effects=True, vmem_limit_bytes=48 * 1024 * 1024),
    )(block_map, queries, key_rows, value_rows, value_turn, block_turn, out_weight)


def solution(mesh):
    placed = (
        P("seq", "head"),
        P("seq", None),
        P("seq", None),
        P(),
        P(),
        P("head", None, None),
        P("head", "seq"),
    )
    return jax.shard_map(
        on_device, mesh=mesh, in_specs=placed, out_specs=P("head", "seq"), check_vma=False
    )
```

time: 613 us -> 149 us (0.24)
  the two profiles are of different devices: /device:TPU:2 before, /device:TPU:24 now
where the time goes in v1:
time: 149 us; the launch traced here: 148 us
  Pallas kernels  141 us (95%)
  local copies, waits for them, and re-layouts  7.24 us (5%)
    pallas_call x1, Pallas kernels, on_device(): pl.pallas_call(kernel, out_shape=jax.ShapeDtypeStruct((256, TOK), BF), in...  141 us
    unnamed x15, local copies, waits for them, and re-layouts  7.24 us

profile of v1, /device:TPU:24, one launch (start us, length us, event | category | flops | bytes accessed | tf_op | source)
XLA Modules:
  0.0 148.2 jit_solution(2534162809730247716)
XLA Ops:
  0.0 0.0 copy-start
  0.0 1.0 copy-done
  1.0 0.0 copy-start.1
  1.0 1.0 copy-done.1
  2.1 0.0 copy-start.2
  2.1 1.0 copy-done.2
  3.1 0.0 copy-start.3
  3.1 0.9 copy-done.3
  4.1 0.0 copy-start.4
  4.1 0.9 copy-done.4
  5.0 0.0 copy-start.5
  5.0 0.9 copy-done.5
  5.9 0.0 copy-start.6
  5.9 0.7 copy-done.6
  6.6 141.0 %shard_map.73 = bf16[256,256]{1,0:T(8,128)(2,1)S(1)} custom-call(s32[128]{0:T(128)S(1)} %copy-done.6, bf16[256,512]{1,0:T(8,128)(2,1)S(1)} %copy-done.3, bf16[256,1024]{1,0:T(8,128)(2,1)S(1)} %copy-done, bf16[256,1024]{1,0:T(8,128)(2,1)S(1)} %copy-done.1, bf16[8,128,128]{2,1,0:T(8,128)(2,1)S(1)} %copy-done.4, bf16[4,128,128]{2,1,0:T(8,128)(2,1)S(1)} %copy-done.5, ...), custom_call_target="tpu_custom_call" | custom-call | tf_op jit(solution)/shard_map/pallas_call | solution.py:316
  147.6 0.7 copy.9
Async XLA Ops:
  0.0 1.0 copy-start
  1.0 1.0 copy-start.1
  2.1 1.0 copy-start.2
  3.1 0.9 copy-start.3
  4.1 0.9 copy-start.4
  5.0 0.9 copy-start.5
  5.9 0.7 copy-start.6

commit v2 on v0

v2 whole, which is shorter than its diff:
```python
import math

import jax
import jax.numpy as jnp
from jax import lax
from jax.experimental import pallas as pl
from jax.experimental.pallas import tpu as pltpu
from jax.sharding import PartitionSpec as P

MESH = pl.DeviceIdType.MESH
BF = jnp.bfloat16
F32 = jnp.float32
HD = 128
TOK = 256
HALF = 128


def dev(zh, x, c, zl, y):
    return (zh * 8 + x * 2 + c, zl * 8 + y)


def send(src, dst, ssem, rsem, to):
    pltpu.make_async_remote_copy(
        src_ref=src, dst_ref=dst, send_sem=ssem, recv_sem=rsem, device_id=to, device_id_type=MESH
    ).start()


def arrived(slot, sem):
    pltpu.make_async_copy(slot, slot, sem).wait()


def kernel(
    map_ref, q_ref, key_ref, val_ref, vturn_ref, bturn_ref, w_ref, out_ref,
    kv, q_all, score, top_ref, total_ref, acc_ref, wst, whop, w1, w2s, wfull, a_st, a_full, cst, cin,
    val_in, vturn_in, w_in, bturn_in, q_in, in_s,
    kc_s, kx_s, kx_r, kc_r, kd_s, kd_r, kxx_s, kxx_r,
    wh_s, wh_r, w1_s, w1_r, w2_s, w2_r, wx_s, wx_r, wd_s, wd_r,
    ac_s, ac_r, rr_s, rr_r, ll_s, ll_r, c_s, c_r,
):
    s = lax.axis_index("seq")
    h = lax.axis_index("head")
    zh, x, c = s // 8, (s // 2) % 4, s % 2
    zl, y = h // 8, h % 8
    z = zh * 4 + zl

    g = zl * 2 + y // 4
    lanes = pl.ds(pl.multiple_of(g * HD, HD), HD)
    load_key = pltpu.make_async_copy(key_ref.at[:, lanes], kv.at[s, 0], in_s.at[0])
    load_val = pltpu.make_async_copy(val_ref.at[:, lanes], val_in, in_s.at[1])
    load_vturn = pltpu.make_async_copy(vturn_ref.at[g], vturn_in, in_s.at[2])
    load_w = pltpu.make_async_copy(w_ref, w_in, in_s.at[3])
    load_bturn = pltpu.make_async_copy(bturn_ref, bturn_in, in_s.at[4])
    load_q = pltpu.make_async_copy(q_ref, q_in, in_s.at[5])
    for load in (load_key, load_val, load_vturn, load_w, load_bturn, load_q):
        load.start()

    w_seq = c * 8 + x * 2 + (y // 2) % 2

    def held_rows(xx, cc):
        hf = (xx + y // 4) % 2
        xs = (xx + 4 - hf) % 4
        return pl.multiple_of((2 * cc + xs // 2) * 256 + hf * 128, 128)

    rows = held_rows(x, c)

    def row16(zq):
        return pl.ds(pl.multiple_of(rows + zq * 16, 16), 16)

    def w1_place(n):
        hf, r, zq = n // 16, (n // 8) % 2, n % 8
        return dev(zq // 4, x, zh, zq % 4, 4 * ((x + hf) % 2) + 2 * c + r)

    chunk = wfull.at[pl.ds(rows, 128), :]
    right = dev(zh, x, c, zl, (y + 1) % 8)
    left = dev(zh, x, c, zl, (y + 7) % 8)

    barrier = pltpu.get_barrier_semaphore()

    def greet(to):
        pl.semaphore_signal(barrier, inc=1, device_id=to, device_id_type=MESH)

    def greet_w1(hh, carry):
        @pl.when(jnp.logical_not((w_seq == s) & (hh == h)))
        def _():
            greet((w_seq, hh))

        return carry

    def entry():
        for d in range(1, 8):
            zt = (z + d) % 8
            greet(dev(zt // 4, x, c, zt % 4, y))
        for off in (1, 2, 3):
            greet(dev(zh, (x + off) % 4, c, zl, y))
        greet(dev(zh, x, 1 - c, zl, y))
        greet(right)
        greet(left)
        lax.fori_loop(0, 32, greet_w1, 0)

    def all_in():
        self_too = (w_seq == s).astype(jnp.int32)
        pl.semaphore_wait(barrier, 45 - self_too)

    def kv_first():
        load_key.wait()
        load_val.wait()
        load_vturn.wait()
        kv[s, 1] = jnp.dot(val_in[...], vturn_in[...], preferred_element_type=F32).astype(BF)

    def kv_send():
        @pl.when(zh == 0)
        def _():
            send(kv.at[s], kv.at[s], kc_s, kc_r, dev(1, x, c, zl, y))

        for off in (1, 2, 3):
            @pl.when(x + off < 4)
            def _():
                send(kv.at[s], kv.at[s], kx_s.at[off], kx_r.at[x], dev(zh, x + off, c, zl, y))

        send(kv.at[s], kv.at[s], kd_s.at[zh * 4 + x], kd_r.at[zh * 4 + x], dev(zh, x, 1 - c, zl, y))

    def w_turn():
        load_w.wait()
        load_bturn.wait()
        for i in range(4):
            turned = lax.dot_general(
                w_in[i * HD:(i + 1) * HD, :], bturn_in[i], (((0,), (1,)), ((), ())), preferred_element_type=F32
            ).astype(BF)
            turned = turned.reshape(32, 16, HD)
            for r in range(2):
                for hf in range(2):
                    wst[hf * 16 + r * 8:hf * 16 + r * 8 + 8, i] = turned[(r * 2 + hf) * 8:(r * 2 + hf) * 8 + 8]

    def w_hop():
        far = wst.at[pl.ds(16, 16)]
        send(far, whop, wh_s, wh_r, dev(zh, (x + 1) % 4, c, zl, y))

    def w1_send(n, src):
        to = w1_place(n)
        mine = (to[0] == s) & (to[1] == h)

        @pl.when(jnp.logical_not(mine))
        def _():
            send(src, w1.at[pl.ds(h * 4, 4)], w1_s.at[n], w1_r.at[h], to)

        @pl.when(mine)
        def _():
            pltpu.make_async_copy(src, w1.at[pl.ds(h * 4, 4)], w1_r.at[h]).start()

    def w_spread():
        def one(step, carry):
            n = (step + h) % 16
            w1_send(n, wst.at[n])
            return carry

        lax.fori_loop(0, 16, one, 0)

    def w_spread_far():
        arrived(whop, wh_r)

        def one(step, carry):
            n = (step + h) % 16
            w1_send(16 + n, whop.at[n])
            return carry

        lax.fori_loop(0, 16, one, 0)

    def kv_second():
        @pl.when(zh == 1)
        def _():
            arrived(kv.at[s - 8], kc_r)
            for off in (1, 3, 2):
                send(kv.at[s - 8], kv.at[s - 8], kxx_s.at[off], kxx_r.at[off], dev(1, (x + off) % 4, c, zl, y))
            send(kv.at[s - 8], kv.at[s - 8], kd_s.at[x], kd_r.at[x], dev(1, x, 1 - c, zl, y))

        for xs in range(3):
            @pl.when(xs < x)
            def _():
                slot = kv.at[zh * 8 + xs * 2 + c]
                arrived(slot, kx_r.at[xs])
                send(slot, slot, kd_s.at[zh * 4 + xs], kd_r.at[zh * 4 + xs], dev(zh, x, 1 - c, zl, y))

        @pl.when(zh == 1)
        def _():
            for off in (1, 3, 2):
                xs = (x + 4 - off) % 4
                slot = kv.at[xs * 2 + c]
                arrived(slot, kxx_r.at[off])
                send(slot, slot, kd_s.at[xs], kd_r.at[xs], dev(1, x, 1 - c, zl, y))

    def kv_wait():
        for xs in range(4):
            @pl.when(xs <= x)
            def _():
                arrived(kv.at[zh * 8 + xs * 2 + 1 - c], kd_r.at[zh * 4 + xs])

            @pl.when(zh == 1)
            def _():
                arrived(kv.at[xs * 2 + 1 - c], kd_r.at[xs])

    def w2_send(step, carry):
        zt = (z + step) % 8
        zht, zlt = zt // 4, zt % 4
        for kk in range(16):
            block = map_ref[(zlt * 8 + kk // 2) * 4 + zht * 2 + kk % 2]
            w2s[step, :, kk * HD:(kk + 1) * HD] = w1[block]

        @pl.when(step > 0)
        def _():
            send(w2s.at[step], wfull.at[row16(z), :], w2_s.at[step], w2_r.at[z], dev(zht, x, c, zlt, y))

        @pl.when(step == 0)
        def _():
            pltpu.make_async_copy(w2s.at[step], wfull.at[row16(z), :], w2_r.at[z]).start()

        return carry

    def w_pick():
        for hh in range(32):
            arrived(w1.at[pl.ds(hh * 4, 4)], w1_r.at[hh])
        lax.fori_loop(0, 8, w2_send, 0)

    def w_gather():
        for d in (0, 1, 7, 2, 6, 3, 5, 4):
            zq = (z + d) % 8
            piece = wfull.at[row16(zq), :]
            arrived(piece, w2_r.at[zq])
            for off in (1, 3):
                send(piece, piece, wx_s.at[off, zq], wx_r.at[off, zq], dev(zh, (x + off) % 4, c, zl, y))
        send(chunk, chunk, wd_s.at[0], wd_r.at[0], dev(zh, x, 1 - c, zl, y))

    def w_share(off):
        base = held_rows((x + 4 - off) % 4, c)
        for zq in range(8):
            piece = wfull.at[pl.ds(pl.multiple_of(base + zq * 16, 16), 16), :]
            arrived(piece, wx_r.at[off, zq])
            if off == 1 and zq < 4 or off == 3 and zq >= 4:
                onward = dev(zh, (x + off) % 4, c, zl, y)
                send(piece, piece, wx_s.at[2, zq], wx_r.at[2, zq], onward)
        theirs = wfull.at[pl.ds(base, 128), :]
        send(theirs, theirs, wd_s.at[off], wd_r.at[off], dev(zh, x, 1 - c, zl, y))

    def w_shared(off):
        base = held_rows((x + 4 - off) % 4, 1 - c)
        arrived(wfull.at[pl.ds(base, 128), :], wd_r.at[off])

    turn = math.log2(math.e) / math.sqrt(HD)
    last = zh * 4 + x

    def attention(t):
        def scored(i, u, j):
            return lax.dot_general(
                q_all[t, i], kv[2 * u + j, 0], (((1,), (1,)), ((), ())), preferred_element_type=F32
            )

        if t == 0:
            load_q.wait()
        for i in range(4):
            q_all[t, i] = q_in[t * HALF:(t + 1) * HALF, i * HD:(i + 1) * HD]
        place = lax.broadcasted_iota(jnp.int32, (HALF, TOK), 0) + (c * TOK + t * HALF)
        key_at = lax.broadcasted_iota(jnp.int32, (HALF, TOK), 1)
        for i in range(4):
            top = None
            for j in range(2):
                value = jnp.where(key_at + j * TOK <= place, scored(i, last, j), F32(-1e30))
                score[last, i, :, j * TOK:(j + 1) * TOK] = value
                value = jnp.maximum(value[:, :HD], value[:, HD:])
                top = value if top is None else jnp.maximum(top, value)
            top_ref[i] = top

        def first(u, carry):
            for i in range(4):
                top = top_ref[i]
                for j in range(2):
                    value = scored(i, u, j)
                    score[u, i, :, j * TOK:(j + 1) * TOK] = value
                    top = jnp.maximum(top, jnp.maximum(value[:, :HD], value[:, HD:]))
                top_ref[i] = top
            return carry

        lax.fori_loop(0, last, first, 0)
        for i in range(4):
            top_ref[i] = jnp.broadcast_to(jnp.max(top_ref[i], axis=1, keepdims=True) * turn, (HALF, HD))
        total_ref[...] = jnp.zeros_like(total_ref)
        acc_ref[...] = jnp.zeros_like(acc_ref)

        def second(u, carry):
            for i in range(4):
                top = top_ref[i]
                total = total_ref[i]
                acc = acc_ref[i]
                for j in range(2):
                    weight = []
                    for k in range(2):
                        lane = j * TOK + k * HD
                        weight.append(jnp.exp2(score[u, i, :, lane:lane + HD] * turn - top))
                        total = total + weight[k]
                    acc = acc + jnp.dot(
                        jnp.concatenate(weight, axis=1).astype(BF), kv[2 * u + j, 1], preferred_element_type=F32
                    )
                total_ref[i] = total
                acc_ref[i] = acc
            return carry

        lax.fori_loop(0, last + 1, second, 0)

        def head(i):
            return (acc_ref[i] / jnp.sum(total_ref[i], axis=1, keepdims=True)).astype(BF)

        for k in range(2):
            @pl.when(zh == k)
            def _():
                for i in range(2):
                    a_full[t, y, zh, :, i * HD:(i + 1) * HD] = head(2 * k + i)
                    a_st[t, :, i * HD:(i + 1) * HD] = head(2 * (1 - k) + i)

    def part(t, slot, p):
        return a_full.at[t, slot % 8, zh if p == 0 else 1 - zh]

    def go(t, k, p):
        if k < 3 or p == 0:
            ref = part(t, y + 8 - k, p)
            send(ref, ref, rr_s.at[t, k, p], rr_r.at[t, k, p], right)
        if k < 3 or p == 1:
            ref = part(t, y + k, p)
            send(ref, ref, ll_s.at[t, k, p], ll_r.at[t, k, p], left)

    def a_start(t):
        send(a_st.at[t], a_full.at[t, y, zh], ac_s.at[t], ac_r.at[t], dev(1 - zh, x, c, zl, y))
        go(t, 0, 0)

    def a_cross(t):
        arrived(part(t, y, 1), ac_r.at[t])
        go(t, 0, 1)

    def a_ring(t, k):
        for p in (0, 1):
            arrived(part(t, y + 8 - k, p), rr_r.at[t, k - 1, p])
            arrived(part(t, y + k, p), ll_r.at[t, k - 1, p])
            go(t, k, p)

    def a_last(t):
        arrived(part(t, y + 4, 0), rr_r.at[t, 3, 0])
        arrived(part(t, y + 4, 1), ll_r.at[t, 3, 1])

    def owner(off, cc):
        base = held_rows((x + 4 - off) % 4, cc)
        return base, base // 256, (base // 128) % 2

    def project(t, off):
        for cc in range(2):
            base, zlt, hf = owner(off, cc)
            acc = jnp.zeros((128, TOK), F32)
            for yy in range(8):
                acc = acc + lax.dot_general(
                    wfull[pl.ds(base, 128), yy * 256:(yy + 1) * 256], a_full[t, yy].reshape(TOK, 256),
                    (((1,), (1,)), ((), ())), preferred_element_type=F32,
                )
            for zht in range(2):
                value = acc[:, zht * HALF:(zht + 1) * HALF].astype(BF)
                mine = (zht == zh) & (zlt == zl)

                @pl.when(mine)
                def _():
                    cin[t, z, hf] = value

                @pl.when(jnp.logical_not(mine))
                def _():
                    piece = cst.at[t, off, cc, zht]
                    piece[...] = value
                    send(piece, cin.at[t, z, hf], c_s.at[t, off, cc, zht], c_r.at[t, z, hf], dev(zht, x, c, zlt, y))

    def collect(t):
        for hf in range(2):
            total = cin[t, z, hf].astype(F32)
            for d in (1, 7, 2, 6, 3, 5, 4):
                zs = (z + d) % 8
                arrived(cin.at[t, zs, hf], c_r.at[t, zs, hf])
                total = total + cin[t, zs, hf].astype(F32)
            out_ref[hf * 128:(hf + 1) * 128, t * HALF:(t + 1) * HALF] = total.astype(BF)

    def kv_drain():
        @pl.when(zh == 0)
        def _():
            arrived(kv.at[s], kc_s)

        for off in (1, 2, 3):
            @pl.when(x + off < 4)
            def _():
                arrived(kv.at[s], kx_s.at[off])

            @pl.when(zh == 1)
            def _():
                arrived(kv.at[s], kxx_s.at[off])

        for xs in range(4):
            @pl.when(xs <= x)
            def _():
                arrived(kv.at[s], kd_s.at[zh * 4 + xs])

            @pl.when(zh == 1)
            def _():
                arrived(kv.at[s], kd_s.at[xs])

    def w_turn_drain():
        def w1_sent(n, carry):
            to = w1_place(n)

            @pl.when(jnp.logical_not((to[0] == s) & (to[1] == h)))
            def _():
                arrived(wst.at[n], w1_s.at[n])

            return carry

        lax.fori_loop(0, 32, w1_sent, 0)

    def w_pick_drain():
        arrived(whop, wh_s)
        for d in range(1, 8):
            arrived(w2s.at[d], w2_s.at[d])

    def w_gather_drain():
        for off in (1, 2, 3):
            for zq in range(8):
                arrived(wfull.at[row16(zq), :], wx_s.at[off, zq])
            arrived(chunk, wd_s.at[off])
        arrived(chunk, wd_s.at[0])

    def a_drain():
        for t in range(2):
            arrived(a_st.at[t], ac_s.at[t])
            for k in range(4):
                for p in (0, 1):
                    if k < 3 or p == 0:
                        arrived(part(t, y, 0), rr_s.at[t, k, p])
                    if k < 3 or p == 1:
                        arrived(part(t, y, 0), ll_s.at[t, k, p])

    def proj_drain():
        for t in range(2):
            for off in range(4):
                for cc in range(2):
                    zlt = owner(off, cc)[1]
                    for zht in range(2):
                        @pl.when(jnp.logical_not((zht == zh) & (zlt == zl)))
                        def _():
                            arrived(cst.at[t, off, cc, zht], c_s.at[t, off, cc, zht])

    entry()
    kv_first()
    all_in()
    kv_send()
    w_turn()
    w_hop()
    w_spread()
    kv_second()
    w_spread_far()
    kv_wait()
    attention(0)
    a_start(0)
    attention(1)
    a_start(1)
    a_cross(0)
    w_pick()
    a_ring(0, 1)
    a_cross(1)
    a_ring(0, 2)
    a_ring(1, 1)
    w_gather()
    a_ring(0, 3)
    a_ring(1, 2)
    a_last(0)
    w_share(1)
    w_share(3)
    w_shared(0)
    project(0, 0)
    a_ring(1, 3)
    w_shared(1)
    project(0, 1)
    w_shared(3)
    project(0, 3)
    a_last(1)
    project(1, 0)
    project(1, 1)
    project(1, 3)
    w_share(2)
    w_shared(2)
    project(0, 2)
    project(1, 2)
    collect(0)
    collect(1)
    kv_drain()
    w_turn_drain()
    w_pick_drain()
    w_gather_drain()
    a_drain()
    proj_drain()


def on_device(queries, key_rows, value_rows, value_turn, block_map, block_turn, out_weight):
    dma = pltpu.SemaphoreType.DMA
    return pl.pallas_call(
        kernel,
        out_shape=jax.ShapeDtypeStruct((256, TOK), BF),
        in_specs=[pl.BlockSpec(memory_space=pltpu.SMEM)] + [pl.BlockSpec(memory_space=pltpu.HBM)] * 6,
        out_specs=pl.BlockSpec(memory_space=pltpu.VMEM),
        scratch_shapes=[
            pltpu.VMEM((16, 2, TOK, HD), BF),
            pltpu.VMEM((2, 4, HALF, HD), BF),
            pltpu.VMEM((8, 4, HALF, 2 * TOK), F32),
            pltpu.VMEM((4, HALF, HD), F32),
            pltpu.VMEM((4, HALF, HD), F32),
            pltpu.VMEM((4, HALF, HD), F32),
            pltpu.VMEM((32, 4, 16, HD), BF),
            pltpu.VMEM((16, 4, 16, HD), BF),
            pltpu.VMEM((128, 16, HD), BF),
            pltpu.VMEM((8, 16, 2048), BF),
            pltpu.VMEM((1024, 2048), BF),
            pltpu.VMEM((2, HALF, 256), BF),
            pltpu.VMEM((2, 8, 2, HALF, 256), BF),
            pltpu.VMEM((2, 4, 2, 2, 128, HALF), BF),
            pltpu.VMEM((2, 8, 2, 128, HALF), BF),
            pltpu.VMEM((TOK, HD), BF),
            pltpu.VMEM((HD, HD), BF),
            pltpu.VMEM((512, 512), BF),
            pltpu.VMEM((4, HD, HD), BF),
            pltpu.VMEM((TOK, 512), BF),
            dma((6,)),
            dma(()), dma((4,)), dma((4,)), dma(()), dma((8,)), dma((8,)), dma((4,)), dma((4,)),
            dma(()), dma(()), dma((32,)), dma((32,)), dma((8,)), dma((8,)), dma((4, 8)), dma((4, 8)), dma((4,)), dma((4,)),
            dma((2,)), dma((2,)), dma((2, 4, 2)), dma((2, 4, 2)), dma((2, 4, 2)), dma((2, 4, 2)),
            dma((2, 4, 2, 2)), dma((2, 8, 2)),
        ],
        compiler_params=pltpu.CompilerParams(
            has_side_effects=True, collective_id=0, vmem_limit_bytes=60 * 1024 * 1024
        ),
    )(block_map, queries, key_rows, value_rows, value_turn, block_turn, out_weight)


def solution(mesh):
    placed = (
        P("seq", "head"),
        P("seq", None),
        P("seq", None),
        P(),
        P(),
        P("head", None, None),
        P("head", "seq"),
    )
    return jax.shard_map(
        on_device, mesh=mesh, in_specs=placed, out_specs=P("head", "seq"), check_vma=False
    )
```

time: 613 us -> 120 us (0.20)
  the two profiles are of different devices: /device:TPU:2 before, /device:TPU:8 now
where the time goes in v2:
time: 120 us; the launch traced here: 119 us
  Pallas kernels  118 us (98%)
  local copies, waits for them, and re-layouts  1.57 us (1%)
    pallas_call x1, Pallas kernels, on_device(): pl.pallas_call(kernel, out_shape=jax.ShapeDtypeStruct((256, TOK), BF), in...  118 us

profile of v2, /device:TPU:8, one launch (start us, length us, event | category | flops | bytes accessed | tf_op | source)
XLA Modules:
  0.0 119.4 jit_solution(12756746757066287134)
XLA Ops:
  0.0 117.8 %shard_map.73 = bf16[256,256]{1,0:T(8,128)(2,1)} custom-call(s32[128]{0:T(128)} %map_ref.1, bf16[256,512]{1,0:T(8,128)(2,1)} %q_ref.1, bf16[256,1024]{1,0:T(8,128)(2,1)} %key_ref.1, bf16[256,1024]{1,0:T(8,128)(2,1)} %val_ref.1, bf16[8,128,128]{2,1,0:T(8,128)(2,1)} %vturn_ref.1, bf16[4,128,128]{2,1,0:T(8,128)(2,1)} %bturn_ref.1, bf16[512,512]{1,0:T(8,128)(2,1)} %w_ref.1), custom_call_target="tpu_custom_call" | custom-call | tf_op jit(solution)/shard_map/pallas_call | solution.py:502
  117.8 1.6 %copy.9 = bf16[256,256]{1,0:T(8,128)(2,1)} copy(bf16[256,256]{1,0:T(8,128)(2,1)} %shard_map.73) | data formatting | bytes 262144

commit v3 on v2

--- a/solution.py
+++ b/solution.py
@@ -54,7 +54,8 @@
     for load in (load_key, load_val, load_vturn, load_w, load_bturn, load_q):
         load.start()
 
-    w_seq = c * 8 + x * 2 + (y // 2) % 2
+    w_seq = zh * 8 + x * 2 + (y // 2) % 2
+    w_at = zl * 2 + c
 
     def held_rows(xx, cc):
         hf = (xx + y // 4) % 2
@@ -63,12 +64,12 @@
 
     rows = held_rows(x, c)
 
-    def row16(zq):
-        return pl.ds(pl.multiple_of(rows + zq * 16, 16), 16)
+    def row16(base, m):
+        return pl.ds(pl.multiple_of(base + m * 16, 16), 16)
 
     def w1_place(n):
-        hf, r, zq = n // 16, (n // 8) % 2, n % 8
-        return dev(zq // 4, x, zh, zq % 4, 4 * ((x + hf) % 2) + 2 * c + r)
+        hf, r, m = n // 16, (n // 8) % 2, n % 8
+        return dev(zh, x, m % 2, m // 2, 4 * ((x + hf) % 2) + 2 * c + r)
 
     chunk = wfull.at[pl.ds(rows, 128), :]
     right = dev(zh, x, c, zl, (y + 1) % 8)
@@ -96,10 +97,15 @@
         greet(right)
         greet(left)
         lax.fori_loop(0, 32, greet_w1, 0)
+        for m in range(8):
+            @pl.when(jnp.logical_not((c == zh) & (m == w_at)))
+            def _():
+                greet(dev(c, x, m % 2, m // 2, y))
+
 
     def all_in():
-        self_too = (w_seq == s).astype(jnp.int32)
-        pl.semaphore_wait(barrier, 45 - self_too)
+        own = (w_seq == s).astype(jnp.int32) + (c == zh).astype(jnp.int32)
+        pl.semaphore_wait(barrier, 53 - own)
 
     def kv_first():
         load_key.wait()
@@ -119,17 +125,17 @@
 
         send(kv.at[s], kv.at[s], kd_s.at[zh * 4 + x], kd_r.at[zh * 4 + x], dev(zh, x, 1 - c, zl, y))
 
-    def w_turn():
-        load_w.wait()
-        load_bturn.wait()
+    def w_turn(hf):
+        if hf == 1:
+            load_w.wait()
+            load_bturn.wait()
         for i in range(4):
-            turned = lax.dot_general(
-                w_in[i * HD:(i + 1) * HD, :], bturn_in[i], (((0,), (1,)), ((), ())), preferred_element_type=F32
-            ).astype(BF)
-            turned = turned.reshape(32, 16, HD)
             for r in range(2):
-                for hf in range(2):
-                    wst[hf * 16 + r * 8:hf * 16 + r * 8 + 8, i] = turned[(r * 2 + hf) * 8:(r * 2 + hf) * 8 + 8]
+                turned = lax.dot_general(
+                    w_in[i * HD:(i + 1) * HD, (2 * r + hf) * 128:(2 * r + hf + 1) * 128], bturn_in[i],
+                    (((0,), (1,)), ((), ())), preferred_element_type=F32,
+                ).astype(BF)
+                wst[hf * 16 + r * 8:hf * 16 + r * 8 + 8, i] = turned.reshape(8, 16, HD)
 
     def w_hop():
         far = wst.at[pl.ds(16, 16)]
@@ -205,13 +211,16 @@
             block = map_ref[(zlt * 8 + kk // 2) * 4 + zht * 2 + kk % 2]
             w2s[step, :, kk * HD:(kk + 1) * HD] = w1[block]
 
-        @pl.when(step > 0)
-        def _():
-            send(w2s.at[step], wfull.at[row16(z), :], w2_s.at[step], w2_r.at[z], dev(zht, x, c, zlt, y))
-
-        @pl.when(step == 0)
-        def _():
-            pltpu.make_async_copy(w2s.at[step], wfull.at[row16(z), :], w2_r.at[z]).start()
+        there = wfull.at[row16(held_rows(x, zh), w_at), :]
+        mine = (step == 0) & (c == zh)
+
+        @pl.when(jnp.logical_not(mine))
+        def _():
+            send(w2s.at[step], there, w2_s.at[step], w2_r.at[w_at], dev(zht, x, zh, zlt, y))
+
+        @pl.when(mine)
+        def _():
+            pltpu.make_async_copy(w2s.at[step], there, w2_r.at[w_at]).start()
 
         return carry
 
@@ -221,12 +230,11 @@
         lax.fori_loop(0, 8, w2_send, 0)
 
     def w_gather():
-        for d in (0, 1, 7, 2, 6, 3, 5, 4):
-            zq = (z + d) % 8
-            piece = wfull.at[row16(zq), :]
-            arrived(piece, w2_r.at[zq])
+        for m in range(8):
+            piece = wfull.at[row16(rows, m), :]
+            arrived(piece, w2_r.at[m])
             for off in (1, 3):
-                send(piece, piece, wx_s.at[off, zq], wx_r.at[off, zq], dev(zh, (x + off) % 4, c, zl, y))
+                send(piece, piece, wx_s.at[off, m], wx_r.at[off, m], dev(zh, (x + off) % 4, c, zl, y))
         send(chunk, chunk, wd_s.at[0], wd_r.at[0], dev(zh, x, 1 - c, zl, y))
 
     def w_share(off):
@@ -419,10 +427,15 @@
         for d in range(1, 8):
             arrived(w2s.at[d], w2_s.at[d])
 
+        @pl.when(c != zh)
+        def _():
+            arrived(w2s.at[0], w2_s.at[0])
+
+
     def w_gather_drain():
         for off in (1, 2, 3):
             for zq in range(8):
-                arrived(wfull.at[row16(zq), :], wx_s.at[off, zq])
+                arrived(wfull.at[row16(rows, zq), :], wx_s.at[off, zq])
             arrived(chunk, wd_s.at[off])
         arrived(chunk, wd_s.at[0])
 
@@ -450,10 +463,11 @@
     kv_first()
     all_in()
     kv_send()
-    w_turn()
+    w_turn(1)
     w_hop()
+    w_turn(0)
+    kv_second()
     w_spread()
-    kv_second()
     w_spread_far()
     kv_wait()
     attention(0)
@@ -487,13 +501,13 @@
     w_shared(2)
     project(0, 2)
     project(1, 2)
-    collect(0)
-    collect(1)
     kv_drain()
     w_turn_drain()
     w_pick_drain()
     w_gather_drain()
     a_drain()
+    collect(0)
+    collect(1)
     proj_drain()
 
 

time: 120 us -> 109 us (0.908)
  the two profiles are of different devices: /device:TPU:8 before, /device:TPU:14 now
where the time goes in v3:
time: 109 us
  Pallas kernels  108 us (99%)
  local copies, waits for them, and re-layouts  1.57 us (1%)
    pallas_call x1, Pallas kernels, on_device(): pl.pallas_call(kernel, out_shape=jax.ShapeDtypeStruct((256, TOK), BF), in...  108 us

profile of v3, /device:TPU:14, one launch (start us, length us, event | category | flops | bytes accessed | tf_op | source)
XLA Modules:
  0.0 109.2 jit_solution(15327126675307330622)
XLA Ops:
  0.0 107.6 %shard_map.73 = bf16[256,256]{1,0:T(8,128)(2,1)} custom-call(s32[128]{0:T(128)} %map_ref.1, bf16[256,512]{1,0:T(8,128)(2,1)} %q_ref.1, bf16[256,1024]{1,0:T(8,128)(2,1)} %key_ref.1, bf16[256,1024]{1,0:T(8,128)(2,1)} %val_ref.1, bf16[8,128,128]{2,1,0:T(8,128)(2,1)} %vturn_ref.1, bf16[4,128,128]{2,1,0:T(8,128)(2,1)} %bturn_ref.1, bf16[512,512]{1,0:T(8,128)(2,1)} %w_ref.1), custom_call_target="tpu_custom_call" | custom-call | tf_op jit(solution)/shard_map/pallas_call | solution.py:516
  107.6 1.6 %copy.9 = bf16[256,256]{1,0:T(8,128)(2,1)} copy(bf16[256,256]{1,0:T(8,128)(2,1)} %shard_map.73) | data formatting | bytes 262144

commit v4 on v3

--- a/solution.py
+++ b/solution.py
@@ -64,6 +64,9 @@
 
     rows = held_rows(x, c)
 
+    def lanes1024(k):
+        return pl.ds(pl.multiple_of(k * 1024, 1024), 1024)
+
     def row16(base, m):
         return pl.ds(pl.multiple_of(base + m * 16, 16), 16)
 
@@ -204,49 +207,51 @@
             def _():
                 arrived(kv.at[xs * 2 + 1 - c], kd_r.at[xs])
 
-    def w2_send(step, carry):
+    def w2_send(n, carry):
+        k, step = n // 8, n % 8
         zt = (z + step) % 8
         zht, zlt = zt // 4, zt % 4
-        for kk in range(16):
-            block = map_ref[(zlt * 8 + kk // 2) * 4 + zht * 2 + kk % 2]
-            w2s[step, :, kk * HD:(kk + 1) * HD] = w1[block]
-
-        there = wfull.at[row16(held_rows(x, zh), w_at), :]
+        for kk in range(8):
+            block = map_ref[(zlt * 8 + k * 4 + kk // 2) * 4 + zht * 2 + kk % 2]
+            w2s[k, step, :, kk * HD:(kk + 1) * HD] = w1[block]
+        src = w2s.at[k, step]
+        there = wfull.at[row16(held_rows(x, zh), w_at), lanes1024(k)]
         mine = (step == 0) & (c == zh)
 
         @pl.when(jnp.logical_not(mine))
         def _():
-            send(w2s.at[step], there, w2_s.at[step], w2_r.at[w_at], dev(zht, x, zh, zlt, y))
+            send(src, there, w2_s.at[k, step], w2_r.at[k, w_at], dev(zht, x, zh, zlt, y))
 
         @pl.when(mine)
         def _():
-            pltpu.make_async_copy(w2s.at[step], there, w2_r.at[w_at]).start()
+            pltpu.make_async_copy(src, there, w2_r.at[k, w_at]).start()
 
         return carry
 
     def w_pick():
         for hh in range(32):
             arrived(w1.at[pl.ds(hh * 4, 4)], w1_r.at[hh])
-        lax.fori_loop(0, 8, w2_send, 0)
-
-    def w_gather():
+        lax.fori_loop(0, 16, w2_send, 0)
+
+    def w_gather(k):
         for m in range(8):
-            piece = wfull.at[row16(rows, m), :]
-            arrived(piece, w2_r.at[m])
+            piece = wfull.at[row16(rows, m), lanes1024(k)]
+            arrived(piece, w2_r.at[k, m])
             for off in (1, 3):
-                send(piece, piece, wx_s.at[off, m], wx_r.at[off, m], dev(zh, (x + off) % 4, c, zl, y))
-        send(chunk, chunk, wd_s.at[0], wd_r.at[0], dev(zh, x, 1 - c, zl, y))
-
-    def w_share(off):
+                send(piece, piece, wx_s.at[off, k, m], wx_r.at[off, k, m], dev(zh, (x + off) % 4, c, zl, y))
+        if k == 1:
+            send(chunk, chunk, wd_s.at[0], wd_r.at[0], dev(zh, x, 1 - c, zl, y))
+
+    def w_relay(off, k):
         base = held_rows((x + 4 - off) % 4, c)
-        for zq in range(8):
-            piece = wfull.at[pl.ds(pl.multiple_of(base + zq * 16, 16), 16), :]
-            arrived(piece, wx_r.at[off, zq])
-            if off == 1 and zq < 4 or off == 3 and zq >= 4:
-                onward = dev(zh, (x + off) % 4, c, zl, y)
-                send(piece, piece, wx_s.at[2, zq], wx_r.at[2, zq], onward)
-        theirs = wfull.at[pl.ds(base, 128), :]
-        send(theirs, theirs, wd_s.at[off], wd_r.at[off], dev(zh, x, 1 - c, zl, y))
+        for m in range(8):
+            piece = wfull.at[row16(base, m), lanes1024(k)]
+            arrived(piece, wx_r.at[off, k, m])
+            if off == 1 and m < 4 or off == 3 and m >= 4:
+                send(piece, piece, wx_s.at[2, k, m], wx_r.at[2, k, m], dev(zh, (x + off) % 4, c, zl, y))
+        if k == 1:
+            theirs = wfull.at[pl.ds(base, 128), :]
+            send(theirs, theirs, wd_s.at[off], wd_r.at[off], dev(zh, x, 1 - c, zl, y))
 
     def w_shared(off):
         base = held_rows((x + 4 - off) % 4, 1 - c)
@@ -424,18 +429,19 @@
 
     def w_pick_drain():
         arrived(whop, wh_s)
-        for d in range(1, 8):
-            arrived(w2s.at[d], w2_s.at[d])
-
-        @pl.when(c != zh)
-        def _():
-            arrived(w2s.at[0], w2_s.at[0])
-
+        for k in range(2):
+            for d in range(1, 8):
+                arrived(w2s.at[k, d], w2_s.at[k, d])
+
+            @pl.when(c != zh)
+            def _():
+                arrived(w2s.at[k, 0], w2_s.at[k, 0])
 
     def w_gather_drain():
         for off in (1, 2, 3):
-            for zq in range(8):
-                arrived(wfull.at[row16(rows, zq), :], wx_s.at[off, zq])
+            for k in range(2):
+                for m in range(8):
+                    arrived(wfull.at[row16(rows, m), lanes1024(k)], wx_s.at[off, k, m])
             arrived(chunk, wd_s.at[off])
         arrived(chunk, wd_s.at[0])
 
@@ -479,15 +485,18 @@
     a_ring(0, 1)
     a_cross(1)
     a_ring(0, 2)
+    w_gather(0)
     a_ring(1, 1)
-    w_gather()
+    w_gather(1)
     a_ring(0, 3)
+    w_relay(1, 0)
+    w_relay(3, 0)
     a_ring(1, 2)
     a_last(0)
-    w_share(1)
-    w_share(3)
     w_shared(0)
     project(0, 0)
+    w_relay(1, 1)
+    w_relay(3, 1)
     a_ring(1, 3)
     w_shared(1)
     project(0, 1)
@@ -497,7 +506,8 @@
     project(1, 0)
     project(1, 1)
     project(1, 3)
-    w_share(2)
+    w_relay(2, 0)
+    w_relay(2, 1)
     w_shared(2)
     project(0, 2)
     project(1, 2)
@@ -528,7 +538,7 @@
             pltpu.VMEM((32, 4, 16, HD), BF),
             pltpu.VMEM((16, 4, 16, HD), BF),
             pltpu.VMEM((128, 16, HD), BF),
-            pltpu.VMEM((8, 16, 2048), BF),
+            pltpu.VMEM((2, 8, 16, 1024), BF),
             pltpu.VMEM((1024, 2048), BF),
             pltpu.VMEM((2, HALF, 256), BF),
             pltpu.VMEM((2, 8, 2, HALF, 256), BF),
@@ -541,7 +551,7 @@
             pltpu.VMEM((TOK, 512), BF),
             dma((6,)),
             dma(()), dma((4,)), dma((4,)), dma(()), dma((8,)), dma((8,)), dma((4,)), dma((4,)),
-            dma(()), dma(()), dma((32,)), dma((32,)), dma((8,)), dma((8,)), dma((4, 8)), dma((4, 8)), dma((4,)), dma((4,)),
+            dma(()), dma(()), dma((32,)), dma((32,)), dma((2, 8)), dma((2, 8)), dma((4, 2, 8)), dma((4, 2, 8)), dma((4,)), dma((4,)),
             dma((2,)), dma((2,)), dma((2, 4, 2)), dma((2, 4, 2)), dma((2, 4, 2)), dma((2, 4, 2)),
             dma((2, 4, 2, 2)), dma((2, 8, 2)),
         ],

time: 109 us -> 105 us (0.963)
  the two profiles are of different devices: /device:TPU:14 before, /device:TPU:39 now
where the time goes in v4:
time: 105 us; the launch traced here: 104 us
  Pallas kernels  103 us (98%)
  local copies, waits for them, and re-layouts  1.57 us (1%)
    pallas_call x1, Pallas kernels, on_device(): pl.pallas_call(kernel, out_shape=jax.ShapeDtypeStruct((256, TOK), BF), in...  103 us

profile of v4, /device:TPU:39, one launch (start us, length us, event | category | flops | bytes accessed | tf_op | source)
XLA Modules:
  0.0 104.4 jit_solution(11247754609363651572)
XLA Ops:
  0.0 102.8 %shard_map.73 = bf16[256,256]{1,0:T(8,128)(2,1)} custom-call(s32[128]{0:T(128)} %map_ref.1, bf16[256,512]{1,0:T(8,128)(2,1)} %q_ref.1, bf16[256,1024]{1,0:T(8,128)(2,1)} %key_ref.1, bf16[256,1024]{1,0:T(8,128)(2,1)} %val_ref.1, bf16[8,128,128]{2,1,0:T(8,128)(2,1)} %vturn_ref.1, bf16[4,128,128]{2,1,0:T(8,128)(2,1)} %bturn_ref.1, bf16[512,512]{1,0:T(8,128)(2,1)} %w_ref.1), custom_call_target="tpu_custom_call" | custom-call | tf_op jit(solution)/shard_map/pallas_call | solution.py:526
  102.8 1.6 %copy.9 = bf16[256,256]{1,0:T(8,128)(2,1)} copy(bf16[256,256]{1,0:T(8,128)(2,1)} %shard_map.73) | data formatting | bytes 262144

commit v5 on v4

--- a/solution.py
+++ b/solution.py
@@ -35,7 +35,7 @@
     val_in, vturn_in, w_in, bturn_in, q_in, in_s,
     kc_s, kx_s, kx_r, kc_r, kd_s, kd_r, kxx_s, kxx_r,
     wh_s, wh_r, w1_s, w1_r, w2_s, w2_r, wx_s, wx_r, wd_s, wd_r,
-    ac_s, ac_r, rr_s, rr_r, ll_s, ll_r, c_s, c_r,
+    ac_s, ac_r, ring_s, rr_r, ll_r, c_s, c_r,
 ):
     s = lax.axis_index("seq")
     h = lax.axis_index("head")
@@ -150,11 +150,11 @@
 
         @pl.when(jnp.logical_not(mine))
         def _():
-            send(src, w1.at[pl.ds(h * 4, 4)], w1_s.at[n], w1_r.at[h], to)
+            send(src, w1.at[pl.ds(h * 4, 4)], w1_s, w1_r, to)
 
         @pl.when(mine)
         def _():
-            pltpu.make_async_copy(src, w1.at[pl.ds(h * 4, 4)], w1_r.at[h]).start()
+            pltpu.make_async_copy(src, w1.at[pl.ds(h * 4, 4)], w1_r).start()
 
     def w_spread():
         def one(step, carry):
@@ -220,35 +220,37 @@
 
         @pl.when(jnp.logical_not(mine))
         def _():
-            send(src, there, w2_s.at[k, step], w2_r.at[k, w_at], dev(zht, x, zh, zlt, y))
+            send(src, there, w2_s, w2_r.at[k], dev(zht, x, zh, zlt, y))
 
         @pl.when(mine)
         def _():
-            pltpu.make_async_copy(src, there, w2_r.at[k, w_at]).start()
+            pltpu.make_async_copy(src, there, w2_r.at[k]).start()
 
         return carry
 
     def w_pick():
-        for hh in range(32):
-            arrived(w1.at[pl.ds(hh * 4, 4)], w1_r.at[hh])
+        arrived(w1, w1_r)
         lax.fori_loop(0, 16, w2_send, 0)
 
     def w_gather(k):
-        for m in range(8):
-            piece = wfull.at[row16(rows, m), lanes1024(k)]
-            arrived(piece, w2_r.at[k, m])
-            for off in (1, 3):
-                send(piece, piece, wx_s.at[off, k, m], wx_r.at[off, k, m], dev(zh, (x + off) % 4, c, zl, y))
+        piece = wfull.at[pl.ds(rows, 128), lanes1024(k)]
+        arrived(piece, w2_r.at[k])
+        for off in (1, 3):
+            send(piece, piece, wx_s.at[off, k], wx_r.at[off, k], dev(zh, (x + off) % 4, c, zl, y))
         if k == 1:
             send(chunk, chunk, wd_s.at[0], wd_r.at[0], dev(zh, x, 1 - c, zl, y))
 
     def w_relay(off, k):
         base = held_rows((x + 4 - off) % 4, c)
-        for m in range(8):
-            piece = wfull.at[row16(base, m), lanes1024(k)]
-            arrived(piece, wx_r.at[off, k, m])
-            if off == 1 and m < 4 or off == 3 and m >= 4:
-                send(piece, piece, wx_s.at[2, k, m], wx_r.at[2, k, m], dev(zh, (x + off) % 4, c, zl, y))
+        upper = wfull.at[pl.ds(base, 64), lanes1024(k)]
+        lower = wfull.at[pl.ds(pl.multiple_of(base + 64, 64), 64), lanes1024(k)]
+        if off == 2:
+            arrived(upper, wx_r.at[2, k])
+            arrived(lower, wx_r.at[0, k])
+        else:
+            arrived(wfull.at[pl.ds(base, 128), lanes1024(k)], wx_r.at[off, k])
+            piece, kind = (upper, 2) if off == 1 else (lower, 0)
+            send(piece, piece, wx_s.at[kind, k], wx_r.at[kind, k], dev(zh, (x + off) % 4, c, zl, y))
         if k == 1:
             theirs = wfull.at[pl.ds(base, 128), :]
             send(theirs, theirs, wd_s.at[off], wd_r.at[off], dev(zh, x, 1 - c, zl, y))
@@ -333,10 +335,10 @@
     def go(t, k, p):
         if k < 3 or p == 0:
             ref = part(t, y + 8 - k, p)
-            send(ref, ref, rr_s.at[t, k, p], rr_r.at[t, k, p], right)
+            send(ref, ref, ring_s.at[t], rr_r.at[t, k, p], right)
         if k < 3 or p == 1:
             ref = part(t, y + k, p)
-            send(ref, ref, ll_s.at[t, k, p], ll_r.at[t, k, p], left)
+            send(ref, ref, ring_s.at[t], ll_r.at[t, k, p], left)
 
     def a_start(t):
         send(a_st.at[t], a_full.at[t, y, zh], ac_s.at[t], ac_r.at[t], dev(1 - zh, x, c, zl, y))
@@ -379,16 +381,17 @@
 
                 @pl.when(jnp.logical_not(mine))
                 def _():
-                    piece = cst.at[t, off, cc, zht]
+                    piece = cst.at[t, off * 4 + cc * 2 + zht]
                     piece[...] = value
-                    send(piece, cin.at[t, z, hf], c_s.at[t, off, cc, zht], c_r.at[t, z, hf], dev(zht, x, c, zlt, y))
+                    send(piece, cin.at[t, z, hf], c_s.at[t], c_r.at[t, z], dev(zht, x, c, zlt, y))
 
     def collect(t):
+        for d in (1, 7, 2, 6, 3, 5, 4):
+            zs = (z + d) % 8
+            arrived(cin.at[t, zs], c_r.at[t, zs])
         for hf in range(2):
-            total = cin[t, z, hf].astype(F32)
-            for d in (1, 7, 2, 6, 3, 5, 4):
-                zs = (z + d) % 8
-                arrived(cin.at[t, zs, hf], c_r.at[t, zs, hf])
+            total = cin[t, 0, hf].astype(F32)
+            for zs in range(1, 8):
                 total = total + cin[t, zs, hf].astype(F32)
             out_ref[hf * 128:(hf + 1) * 128, t * HALF:(t + 1) * HALF] = total.astype(BF)
 
@@ -416,54 +419,38 @@
                 arrived(kv.at[s], kd_s.at[xs])
 
     def w_turn_drain():
-        def w1_sent(n, carry):
-            to = w1_place(n)
-
-            @pl.when(jnp.logical_not((to[0] == s) & (to[1] == h)))
-            def _():
-                arrived(wst.at[n], w1_s.at[n])
-
-            return carry
-
-        lax.fori_loop(0, 32, w1_sent, 0)
+        @pl.when(w_seq == s)
+        def _():
+            arrived(wst.at[pl.ds(0, 31)], w1_s)
+
+        @pl.when(w_seq != s)
+        def _():
+            arrived(wst, w1_s)
 
     def w_pick_drain():
         arrived(whop, wh_s)
-        for k in range(2):
-            for d in range(1, 8):
-                arrived(w2s.at[k, d], w2_s.at[k, d])
-
-            @pl.when(c != zh)
-            def _():
-                arrived(w2s.at[k, 0], w2_s.at[k, 0])
+        @pl.when(c != zh)
+        def _():
+            arrived(w2s, w2_s)
+
+        @pl.when(c == zh)
+        def _():
+            arrived(w2s.at[:, pl.ds(0, 7)], w2_s)
 
     def w_gather_drain():
-        for off in (1, 2, 3):
+        for off in range(4):
             for k in range(2):
-                for m in range(8):
-                    arrived(wfull.at[row16(rows, m), lanes1024(k)], wx_s.at[off, k, m])
+                arrived(wfull.at[pl.ds(rows, 128 if off % 2 else 64), lanes1024(k)], wx_s.at[off, k])
             arrived(chunk, wd_s.at[off])
-        arrived(chunk, wd_s.at[0])
 
     def a_drain():
         for t in range(2):
             arrived(a_st.at[t], ac_s.at[t])
-            for k in range(4):
-                for p in (0, 1):
-                    if k < 3 or p == 0:
-                        arrived(part(t, y, 0), rr_s.at[t, k, p])
-                    if k < 3 or p == 1:
-                        arrived(part(t, y, 0), ll_s.at[t, k, p])
+            arrived(a_full.at[t, pl.ds(0, 7)], ring_s.at[t])
 
     def proj_drain():
         for t in range(2):
-            for off in range(4):
-                for cc in range(2):
-                    zlt = owner(off, cc)[1]
-                    for zht in range(2):
-                        @pl.when(jnp.logical_not((zht == zh) & (zlt == zl)))
-                        def _():
-                            arrived(cst.at[t, off, cc, zht], c_s.at[t, off, cc, zht])
+            arrived(cst.at[t, pl.ds(0, 14)], c_s.at[t])
 
     entry()
     kv_first()
@@ -542,7 +529,7 @@
             pltpu.VMEM((1024, 2048), BF),
             pltpu.VMEM((2, HALF, 256), BF),
             pltpu.VMEM((2, 8, 2, HALF, 256), BF),
-            pltpu.VMEM((2, 4, 2, 2, 128, HALF), BF),
+            pltpu.VMEM((2, 16, 128, HALF), BF),
             pltpu.VMEM((2, 8, 2, 128, HALF), BF),
             pltpu.VMEM((TOK, HD), BF),
             pltpu.VMEM((HD, HD), BF),
@@ -551,9 +538,8 @@
             pltpu.VMEM((TOK, 512), BF),
             dma((6,)),
             dma(()), dma((4,)), dma((4,)), dma(()), dma((8,)), dma((8,)), dma((4,)), dma((4,)),
-            dma(()), dma(()), dma((32,)), dma((32,)), dma((2, 8)), dma((2, 8)), dma((4, 2, 8)), dma((4, 2, 8)), dma((4,)), dma((4,)),
-            dma((2,)), dma((2,)), dma((2, 4, 2)), dma((2, 4, 2)), dma((2, 4, 2)), dma((2, 4, 2)),
-            dma((2, 4, 2, 2)), dma((2, 8, 2)),
+            dma(()), dma(()), dma(()), dma(()), dma(()), dma((2,)), dma((4, 2)), dma((4, 2)), dma((4,)), dma((4,)),
+            dma((2,)), dma((2,)), dma((2,)), dma((2, 4, 2)), dma((2, 4, 2)), dma((2,)), dma((2, 8)),
         ],
         compiler_params=pltpu.CompilerParams(
             has_side_effects=True, collective_id=0, vmem_limit_bytes=60 * 1024 * 1024

time: 105 us -> 103 us (0.981)
  the two profiles are of different devices: /device:TPU:39 before, /device:TPU:75 now
where the time goes in v5:
time: 103 us
  Pallas kernels  101 us (98%)
  local copies, waits for them, and re-layouts  1.57 us (2%)
    pallas_call x1, Pallas kernels, on_device(): pl.pallas_call(kernel, out_shape=jax.ShapeDtypeStruct((256, TOK), BF), in...  101 us

profile of v5, /device:TPU:75, one launch (start us, length us, event | category | flops | bytes accessed | tf_op | source)
XLA Modules:
  0.0 102.6 jit_solution(6045618554558151917)
XLA Ops:
  0.0 101.1 %shard_map.73 = bf16[256,256]{1,0:T(8,128)(2,1)} custom-call(s32[128]{0:T(128)} %map_ref.1, bf16[256,512]{1,0:T(8,128)(2,1)} %q_ref.1, bf16[256,1024]{1,0:T(8,128)(2,1)} %key_ref.1, bf16[256,1024]{1,0:T(8,128)(2,1)} %val_ref.1, bf16[8,128,128]{2,1,0:T(8,128)(2,1)} %vturn_ref.1, bf16[4,128,128]{2,1,0:T(8,128)(2,1)} %bturn_ref.1, bf16[512,512]{1,0:T(8,128)(2,1)} %w_ref.1), custom_call_target="tpu_custom_call" | custom-call | tf_op jit(solution)/shard_map/pallas_call | solution.py:513
  101.1 1.6 %copy.9 = bf16[256,256]{1,0:T(8,128)(2,1)} copy(bf16[256,256]{1,0:T(8,128)(2,1)} %shard_map.73) | data formatting | bytes 262144

commit v6 on v5

--- a/solution.py
+++ b/solution.py
@@ -51,8 +51,6 @@
     load_w = pltpu.make_async_copy(w_ref, w_in, in_s.at[3])
     load_bturn = pltpu.make_async_copy(bturn_ref, bturn_in, in_s.at[4])
     load_q = pltpu.make_async_copy(q_ref, q_in, in_s.at[5])
-    for load in (load_key, load_val, load_vturn, load_w, load_bturn, load_q):
-        load.start()
 
     w_seq = zh * 8 + x * 2 + (y // 2) % 2
     w_at = zl * 2 + c
@@ -208,7 +206,9 @@
                 arrived(kv.at[xs * 2 + 1 - c], kd_r.at[xs])
 
     def w2_send(n, carry):
-        k, step = n // 8, n % 8
+        k, turn_at = n // 8, n % 8
+        far = (turn_at + 1) // 2
+        step = jnp.where(turn_at % 2 == 1, 4 + far, 12 - far) % 8
         zt = (z + step) % 8
         zht, zlt = zt // 4, zt % 4
         for kk in range(8):
@@ -453,6 +453,8 @@
             arrived(cst.at[t, pl.ds(0, 14)], c_s.at[t])
 
     entry()
+    for load in (load_key, load_val, load_vturn, load_w, load_bturn, load_q):
+        load.start()
     kv_first()
     all_in()
     kv_send()

time: 103 us -> 103 us (level)
  the two profiles are of different devices: /device:TPU:75 before, /device:TPU:14 now
where the time goes in v6:
time: 103 us; the launch traced here: 102 us
  Pallas kernels  101 us (98%)
  local copies, waits for them, and re-layouts  1.57 us (2%)
    pallas_call x1, Pallas kernels, on_device(): pl.pallas_call(kernel, out_shape=jax.ShapeDtypeStruct((256, TOK), BF), in...  101 us

profile of v6, /device:TPU:14, one launch (start us, length us, event | category | flops | bytes accessed | tf_op | source)
XLA Modules:
  0.0 102.3 jit_solution(6746330740338730479)
XLA Ops:
  0.0 100.7 %shard_map.73 = bf16[256,256]{1,0:T(8,128)(2,1)} custom-call(s32[128]{0:T(128)} %map_ref.1, bf16[256,512]{1,0:T(8,128)(2,1)} %q_ref.1, bf16[256,1024]{1,0:T(8,128)(2,1)} %key_ref.1, bf16[256,1024]{1,0:T(8,128)(2,1)} %val_ref.1, bf16[8,128,128]{2,1,0:T(8,128)(2,1)} %vturn_ref.1, bf16[4,128,128]{2,1,0:T(8,128)(2,1)} %bturn_ref.1, bf16[512,512]{1,0:T(8,128)(2,1)} %w_ref.1), custom_call_target="tpu_custom_call" | custom-call | tf_op jit(solution)/shard_map/pallas_call | solution.py:515
  100.7 1.6 %copy.9 = bf16[256,256]{1,0:T(8,128)(2,1)} copy(bf16[256,256]{1,0:T(8,128)(2,1)} %shard_map.73) | data formatting | bytes 262144
